TPU v7x, 128 devices: a whole 4x4x4 slice. The times are simulated.
128 devices in a mesh: dp: 32 (over x_hi, y, z), tensor: 4 (over x_lo, core).
Axes of the slice: x: 4 (x_hi: 2, x_lo: 2; x = x_hi * 2 + x_lo), y: 4, z: 4, core: 2. Of those that a mesh axis runs over, the one named last changes fastest.
Arguments:
- inputs: bfloat16 [32768, 640], P('dp'), may hold values from -6 to 6
- segments: int32 [32768], P('dp'), may hold values from 0 to 63, never falling along the last dimension, each value on 1 to 2048 neighbouring positions
- positions: int32 [32768], P('dp'), may hold values from 0 to 2047
- cotangent: bfloat16 [32768, 640], P('dp'), may hold values from -6 to 6
- w_query: bfloat16 [640, 1024], P(None, 'tensor'), may hold values from -0.25 to 0.25
- w_key: bfloat16 [640, 256], replicated, may hold values from -0.25 to 0.25
- w_value: bfloat16 [640, 256], replicated, may hold values from -0.25 to 0.25
- w_out: bfloat16 [1024, 640], P('tensor'), may hold values from -0.1875 to 0.1875
- w_gate: bfloat16 [640, 2048], P(None, 'tensor'), may hold values from -0.25 to 0.25
- w_up: bfloat16 [640, 2048], P(None, 'tensor'), may hold values from -0.25 to 0.25
- w_down: bfloat16 [2048, 640], P('tensor'), may hold values from -0.125 to 0.125
- g_attn_in: float32 [640], replicated, may hold values from 0.1 to 1.9
- g_attn_out: float32 [640], replicated, may hold values from 0.1 to 1.9
- g_ffn_in: float32 [640], replicated, may hold values from 0.1 to 1.9
- g_ffn_out: float32 [640], replicated, may hold values from 0.1 to 1.9
- g_query: float32 [256], replicated, may hold values from 0.1 to 1.9
- g_key: float32 [256], replicated, may hold values from 0.1 to 1.9
Outputs:
- output: bfloat16 [32768, 640], P('dp')
- input_grad: bfloat16 [32768, 640], P('dp')
- grad_query: float32 [640, 1024], P(None, 'tensor')
- grad_key: float32 [640, 256], replicated
- grad_value: float32 [640, 256], replicated
- grad_out: float32 [1024, 640], P('tensor')
- grad_gate: float32 [640, 2048], P(None, 'tensor')
- grad_up: float32 [640, 2048], P(None, 'tensor')
- grad_down: float32 [2048, 640], P('tensor')
- grad_attn_in: float32 [640], replicated
- grad_attn_out: float32 [640], replicated
- grad_ffn_in: float32 [640], replicated
- grad_ffn_out: float32 [640], replicated
- grad_qnorm: float32 [256], replicated
- grad_knorm: float32 [256], replicated
Inputs may be any that keep to these rules, and one draw needn't show every extreme that they name: `segments`: document numbers never fall along the tokens; a document holds at most 2048 tokens.
All inputs are finite; a program needn't handle non-finite values.
Results may differ from a plain program's by a relative error of at most 0.03.
Values may be sent and summed in bfloat16 or wider, within the bound.
A program may use at most 128 MiB of HBM per device.

v0:
```python
import math
import jax
import jax.numpy as jnp
from jax import lax
from jax.sharding import PartitionSpec as P

WINDOW = 512
LENGTH = 1024
EPSILON = 1e-06
ROPE_BASE = 10000.0
NEG_LARGE = -1e30


def in_blocks(x, dim, size):
    before, after = (x.shape[:dim], x.shape[dim + 1 :])
    return jnp.moveaxis(x.reshape(*before, size, -1, *after), dim, 0)


def sum_at_owner(x, axis, dim):
    size = lax.axis_size(axis)
    tiles = lax.all_to_all(in_blocks(x, dim, size), axis, 0, 0, tiled=True)
    return jnp.sum(tiles.astype(jnp.float32), axis=0)


def in_order(tiles, dim):
    tiles = jnp.moveaxis(tiles, 0, dim)
    lengths = tiles.shape
    return tiles.reshape(*lengths[:dim], lengths[dim] * lengths[dim + 1], *lengths[dim + 2 :])


def copy_for_each(x, axis):
    copies = jnp.broadcast_to(x, (lax.axis_size(axis), *x.shape))
    return lax.all_to_all(copies, axis, split_axis=0, concat_axis=0, tiled=True)


def collect(x, axis, dim):
    return in_order(copy_for_each(x, axis), dim)


def in_one_piece(arrays, axis, dim, along):
    both = jnp.concatenate(arrays, axis=along)
    out, at, gathered = (lax.all_gather(both, axis, axis=dim, tiled=True), 0, [])
    for a in arrays:
        gathered.append(lax.slice_in_dim(out, at, at + a.shape[along], axis=along))
        at += a.shape[along]
    return tuple(gathered)


def rms_scale(values, gain_vec):
    return (
        values * lax.rsqrt(jnp.mean(values * values, axis=-1, keepdims=True) + EPSILON) * gain_vec
    )


def gain_term(values, grad_vec):
    scaled = values * lax.rsqrt(jnp.mean(values * values, axis=-1, keepdims=True) + EPSILON)
    return jnp.sum(grad_vec * scaled, axis=0)


def rope_tables(positions, head_size):
    half_size = head_size // 2
    inv_freq = ROPE_BASE ** (-2.0 * jnp.arange(half_size, dtype=jnp.float32) / head_size)
    angles = positions.astype(jnp.float32)[:, None] * inv_freq[None, :]
    return (jnp.cos(angles), jnp.sin(angles))


def rotate(values, cosine, sine_table):
    half_size = values.shape[-1] // 2
    first_half = values[..., :half_size]
    second_half = values[..., half_size:]
    return jnp.concatenate(
        [
            first_half * cosine - second_half * sine_table,
            second_half * cosine + first_half * sine_table,
        ],
        axis=-1,
    )


def rotary_norm(raw_vec, gain_vec, cosine, sine_table):
    return rotate(rms_scale(raw_vec, gain_vec), cosine, sine_table)


def windows(blocks, fill_value):
    earlier = jnp.concatenate([jnp.full_like(blocks[:, :1], fill_value), blocks[:, :-1]], axis=1)
    return jnp.concatenate([earlier, blocks], axis=2)


def unwindow(grads, width):
    front_half = grads[:, :, :width]
    back_half = grads[:, :, width:]
    shifted = jnp.concatenate([front_half[:, 1:], jnp.zeros_like(front_half[:, :1])], axis=1)
    return back_half + shifted


def allowed_mask(seg_rows, seg_keys, width):
    row_ids = lax.broadcasted_iota(jnp.int32, (width, 2 * width), 0)
    key_ids = lax.broadcasted_iota(jnp.int32, (width, 2 * width), 1)
    in_window = (key_ids > row_ids) & (key_ids <= row_ids + width)
    return in_window & (seg_rows[:, None] == seg_keys[None, :])


def block_forward(block_item, score_scale):
    q_block, k_window, v_window, seg_rows, seg_keys = block_item
    width = q_block.shape[1]
    scores = (
        jnp.einsum("hqd,kd->hqk", q_block, k_window, preferred_element_type=jnp.float32)
        * score_scale
    )
    allowed = allowed_mask(seg_rows, seg_keys, width)[None]
    masked = jnp.where(allowed, scores, NEG_LARGE)
    row_max = jnp.max(masked, axis=-1, keepdims=True)
    expo_terms = jnp.where(allowed, jnp.exp(masked - row_max), 0.0)
    row_total = jnp.sum(expo_terms, axis=-1, keepdims=True)
    prob_low = (expo_terms / row_total).astype(jnp.bfloat16)
    block_out = jnp.einsum("hqk,kd->hqd", prob_low, v_window, preferred_element_type=jnp.float32)
    return (block_out, (row_max + jnp.log(row_total))[..., 0])


def block_backward(block_item, score_scale):
    q_block, k_window, v_window, seg_rows, seg_keys, log_totals, grad_block = block_item
    width = q_block.shape[1]
    scores = (
        jnp.einsum("hqd,kd->hqk", q_block, k_window, preferred_element_type=jnp.float32)
        * score_scale
    )
    allowed = allowed_mask(seg_rows, seg_keys, width)[None]
    prob_full = jnp.where(allowed, jnp.exp(scores - log_totals[..., None]), 0.0)
    grad_prob = jnp.einsum("hqd,kd->hqk", grad_block, v_window, preferred_element_type=jnp.float32)
    row_dot = jnp.sum(prob_full * grad_prob, axis=-1, keepdims=True)
    grad_scores = (prob_full * (grad_prob - row_dot)).astype(jnp.bfloat16)
    grad_q = (
        jnp.einsum("hqk,kd->hqd", grad_scores, k_window, preferred_element_type=jnp.float32)
        * score_scale
    )
    grad_k = (
        jnp.einsum("hqk,hqd->kd", grad_scores, q_block, preferred_element_type=jnp.float32)
        * score_scale
    )
    grad_v = jnp.einsum(
        "hqk,hqd->kd",
        prob_full.astype(jnp.bfloat16),
        grad_block,
        preferred_element_type=jnp.float32,
    )
    return (grad_q, grad_k, grad_v)


def local(
    inputs,
    segments,
    positions,
    cotangent,
    w_query,
    w_key,
    w_value,
    w_out,
    w_gate,
    w_up,
    w_down,
    g_attn_in,
    g_attn_out,
    g_ffn_in,
    g_ffn_out,
    g_query,
    g_key,
):
    row_count = inputs.shape[0]
    head_size = w_key.shape[1]
    heads_here = w_query.shape[1] // head_size
    seqs_here = row_count // LENGTH
    blocks_per = LENGTH // WINDOW
    block_total = seqs_here * blocks_per
    score_scale = 1.0 / math.sqrt(head_size)
    share_rows = row_count // lax.axis_size("tensor")
    first_row = lax.axis_index("tensor") * share_rows

    def my_rows(values):
        return lax.dynamic_slice_in_dim(values, first_row, share_rows, 0)

    whole_x = inputs.astype(jnp.float32)
    normed = rms_scale(whole_x, g_attn_in).astype(jnp.bfloat16)
    query_raw = jnp.dot(normed, w_query, preferred_element_type=jnp.float32)
    key_raw = jnp.dot(normed, w_key, preferred_element_type=jnp.float32)
    value_raw = jnp.dot(normed, w_value, preferred_element_type=jnp.float32)
    cosine, sine_table = rope_tables(positions, head_size)
    query_heads = query_raw.reshape(row_count, heads_here, head_size).transpose(1, 0, 2)
    q_rot, q_pull = jax.vjp(
        lambda raw_vec, gain_vec: rotary_norm(raw_vec, gain_vec, cosine, sine_table),
        query_heads,
        g_query,
    )
    k_rot, k_pull = jax.vjp(
        lambda raw_vec, gain_vec: rotary_norm(raw_vec, gain_vec, cosine, sine_table), key_raw, g_key
    )
    q_blocks = (
        q_rot.astype(jnp.bfloat16)
        .reshape(heads_here, block_total, WINDOW, head_size)
        .transpose(1, 0, 2, 3)
    )
    k_windows = windows(
        k_rot.astype(jnp.bfloat16).reshape(seqs_here, blocks_per, WINDOW, head_size), 0
    ).reshape(block_total, 2 * WINDOW, head_size)
    v_windows = windows(
        value_raw.astype(jnp.bfloat16).reshape(seqs_here, blocks_per, WINDOW, head_size), 0
    ).reshape(block_total, 2 * WINDOW, head_size)
    seg_rows = segments.reshape(block_total, WINDOW)
    seg_keys = windows(segments.reshape(seqs_here, blocks_per, WINDOW), -1).reshape(
        block_total, 2 * WINDOW
    )
    block_items = (q_blocks, k_windows, v_windows, seg_rows, seg_keys)
    heads_out, log_totals = lax.map(
        lambda block_item: block_forward(block_item, score_scale), block_items
    )
    heads_low = (
        heads_out.astype(jnp.bfloat16)
        .transpose(0, 2, 1, 3)
        .reshape(row_count, heads_here * head_size)
    )
    attn_term = jnp.dot(heads_low, w_out, preferred_element_type=jnp.float32)
    attn_sum = sum_at_owner(attn_term.astype(jnp.bfloat16), "tensor", 0)
    x_rows = my_rows(whole_x)
    attn_norm, attn_pull = jax.vjp(lambda values: rms_scale(values, g_attn_out), attn_sum)
    mid_rows = x_rows + attn_norm
    ffn_in, ffn_pull = jax.vjp(lambda values: rms_scale(values, g_ffn_in), mid_rows)
    ffn_low = collect(ffn_in.astype(jnp.bfloat16), "tensor", 0)
    gate_raw = jnp.dot(ffn_low, w_gate, preferred_element_type=jnp.float32)
    up_raw = jnp.dot(ffn_low, w_up, preferred_element_type=jnp.float32)
    hidden_full, act_pull = jax.vjp(
        lambda gate_in, up_in: jax.nn.gelu(gate_in, approximate=True) * up_in, gate_raw, up_raw
    )
    hidden = hidden_full.astype(jnp.bfloat16)
    ffn_term = jnp.dot(hidden, w_down, preferred_element_type=jnp.float32)
    ffn_sum = sum_at_owner(ffn_term.astype(jnp.bfloat16), "tensor", 0)
    cot_rows = my_rows(cotangent).astype(jnp.float32)
    out_norm, out_pull = jax.vjp(lambda values: rms_scale(values, g_ffn_out), ffn_sum)
    result = mid_rows + out_norm
    grad_ffn = out_pull(cot_rows)[0]
    output, grad_ffn_low = in_one_piece(
        (result.astype(jnp.bfloat16), grad_ffn.astype(jnp.bfloat16)), "tensor", 0, 1
    )
    grad_hidden = jnp.einsum("rd,fd->rf", grad_ffn_low, w_down, preferred_element_type=jnp.float32)
    grad_down = jnp.einsum("rf,rd->fd", hidden, grad_ffn_low, preferred_element_type=jnp.float32)
    grad_gate_full, grad_up_full = act_pull(grad_hidden)
    grad_gate_low = grad_gate_full.astype(jnp.bfloat16)
    grad_up_low = grad_up_full.astype(jnp.bfloat16)
    grad_gate = jnp.einsum("rd,rf->df", ffn_low, grad_gate_low, preferred_element_type=jnp.float32)
    grad_up = jnp.einsum("rd,rf->df", ffn_low, grad_up_low, preferred_element_type=jnp.float32)
    ffn_in_term = jnp.einsum(
        "rf,df->rd", grad_gate_low, w_gate, preferred_element_type=jnp.float32
    ) + jnp.einsum("rf,df->rd", grad_up_low, w_up, preferred_element_type=jnp.float32)
    ffn_in_grad = sum_at_owner(ffn_in_term.astype(jnp.bfloat16), "tensor", 0)
    grad_mid = cot_rows + ffn_pull(ffn_in_grad)[0]
    grad_attn = attn_pull(grad_mid)[0]
    grad_attn_low = collect(grad_attn.astype(jnp.bfloat16), "tensor", 0)
    grad_out = jnp.einsum("rh,rd->hd", heads_low, grad_attn_low, preferred_element_type=jnp.float32)
    grad_heads = jnp.einsum(
        "rd,hd->rh", grad_attn_low, w_out, preferred_element_type=jnp.float32
    ).astype(jnp.bfloat16)
    grad_blocks = grad_heads.reshape(block_total, WINDOW, heads_here, head_size).transpose(
        0, 2, 1, 3
    )
    grad_qb, grad_kw, grad_vw = lax.map(
        lambda block_item: block_backward(block_item, score_scale),
        block_items + (log_totals, grad_blocks),
    )
    grad_q_rot = grad_qb.transpose(1, 0, 2, 3).reshape(heads_here, row_count, head_size)
    grad_k_rot = unwindow(
        grad_kw.reshape(seqs_here, blocks_per, 2 * WINDOW, head_size), WINDOW
    ).reshape(row_count, head_size)
    grad_v_full = unwindow(
        grad_vw.reshape(seqs_here, blocks_per, 2 * WINDOW, head_size), WINDOW
    ).reshape(row_count, head_size)
    grad_query_raw, grad_qnorm = q_pull(grad_q_rot)
    grad_key_raw, grad_knorm = k_pull(grad_k_rot)
    grad_q_low = (
        grad_query_raw.transpose(1, 0, 2)
        .reshape(row_count, heads_here * head_size)
        .astype(jnp.bfloat16)
    )
    grad_k_low = grad_key_raw.astype(jnp.bfloat16)
    grad_v_low = grad_v_full.astype(jnp.bfloat16)
    grad_query = jnp.einsum("rd,rh->dh", normed, grad_q_low, preferred_element_type=jnp.float32)
    grad_key = jnp.einsum("rd,rh->dh", normed, grad_k_low, preferred_element_type=jnp.float32)
    grad_value = jnp.einsum("rd,rh->dh", normed, grad_v_low, preferred_element_type=jnp.float32)
    input_term = jnp.einsum("rh,dh->rd", grad_q_low, w_query, preferred_element_type=jnp.float32)
    input_term = input_term + jnp.einsum(
        "rh,dh->rd", grad_k_low, w_key, preferred_element_type=jnp.float32
    )
    input_term = input_term + jnp.einsum(
        "rh,dh->rd", grad_v_low, w_value, preferred_element_type=jnp.float32
    )
    input_sum = sum_at_owner(input_term.astype(jnp.bfloat16), "tensor", 0)
    x_grad_norm = jax.vjp(lambda values: rms_scale(values, g_attn_in), x_rows)[1](input_sum)[0]
    grad_rows = grad_mid + x_grad_norm
    gain_inputs = (x_rows, input_sum, attn_sum, grad_mid, mid_rows, ffn_in_grad, ffn_sum, cot_rows)
    input_grad = collect(grad_rows.astype(jnp.bfloat16), "tensor", 0)
    grad_attn_in = gain_term(gain_inputs[0], gain_inputs[1])
    grad_attn_out = gain_term(gain_inputs[2], gain_inputs[3])
    grad_ffn_in = gain_term(gain_inputs[4], gain_inputs[5])
    grad_ffn_out = gain_term(gain_inputs[6], gain_inputs[7])
    grad_query, grad_out, grad_gate, grad_up, grad_down = (
        lax.psum(grad_query.astype(jnp.bfloat16), "dp").astype(jnp.float32),
        lax.psum(grad_out.astype(jnp.bfloat16), "dp").astype(jnp.float32),
        lax.psum(grad_gate.astype(jnp.bfloat16), "dp").astype(jnp.float32),
        lax.psum(grad_up.astype(jnp.bfloat16), "dp").astype(jnp.float32),
        lax.psum(grad_down.astype(jnp.bfloat16), "dp").astype(jnp.float32),
    )
    summed_all = lax.psum(
        (
            grad_key,
            grad_value,
            grad_attn_in,
            grad_attn_out,
            grad_ffn_in,
            grad_ffn_out,
            grad_qnorm,
            grad_knorm,
        ),
        ("dp", "tensor"),
    )
    return (
        output,
        input_grad,
        grad_query,
        summed_all[0],
        summed_all[1],
        grad_out,
        grad_gate,
        grad_up,
        grad_down,
        summed_all[2],
        summed_all[3],
        summed_all[4],
        summed_all[5],
        summed_all[6],
        summed_all[7],
    )


def solution(mesh):
    placed = (
        P("dp", None),
        P("dp"),
        P("dp"),
        P("dp", None),
        P(None, "tensor"),
        P(),
        P(),
        P("tensor", None),
        P(None, "tensor"),
        P(None, "tensor"),
        P("tensor", None),
        P(),
        P(),
        P(),
        P(),
        P(),
        P(),
    )
    return jax.shard_map(
        local,
        mesh=mesh,
        in_specs=placed,
        out_specs=(
            P("dp", None),
            P("dp", None),
            P(None, "tensor"),
            P(),
            P(),
            P("tensor", None),
            P(None, "tensor"),
            P(None, "tensor"),
            P("tensor", None),
            P(),
            P(),
            P(),
            P(),
            P(),
            P(),
        ),
        check_vma=False,
    )
```

profile of v0, /device:TPU:1, one launch (start us, length us, event | category | flops | bytes accessed | tf_op | source)
XLA Modules:
  0.0 761.8 jit_solution(5090513711252032929)
XLA Ops:
  9.4 1.6 multiply_reduce_fusion.1
  11.1 2.1 convolution_convert_fusion.6
  15.2 2.4 fusion.97
  17.9 2.4 fusion.91
  20.3 1.1 fusion.60
  22.3 10.3 %while.28 = (s32[]{:T(128)}, bf16[2,1,512,256]{3,2,1,0:T(8,128)(2,1)S(1)}, f32[2,1,512]{2,1,0:T(1,128)}, s32[2,512]{1,0:T(2,128)S(1)}, s32[2,1024]{1,0:T(2,128)S...) while((s32[]{:T(128)}, ...), condition=%wide.region_6.7_spmd.clone, body=%wide.region_3.6_spmd.sunk.clone | while | flops 552075264 | bytes 8220833 | solution.py:212
  22.3 2.0 fusion.189
  24.3 1.0 fusion.190
  25.3 1.4 fusion.191
  27.5 2.0 fusion.189
  29.5 1.0 fusion.190
  30.5 1.4 fusion.191
  32.6 2.6 convolution_convert_fusion
  35.2 5.7 all-to-all-start
  40.9 1.6 convert_element_type.144
  42.5 14.9 %all-to-all-done = bf16[4,256,640]{2,1,0:T(8,128)(2,1)} async-done(((bf16[4,256,640]{2,1,0:T(8,128)(2,1)}), bf16[4,256,640]{2,1,0:T(8,128)(2,1)}, u32[]{:S(2)}, u32[]{:S(2)}) %all-to-all-start) | async-done | bytes 1310752 | tf_op jit(solution)/shard_map/all_to_all | solution.py:21
  57.4 1.6 convert_reduce_fusion.3
  59.6 2.0 multiply_reduce_fusion.14
  62.4 19.7 %all_to_all.35 = bf16[4,256,640]{2,1,0:T(8,128)(2,1)S(1)} all-to-all(bf16[4,256,640]{2,1,0:T(8,128)(2,1)S(1)} %broadcast_in_dim.57), channel_id=1, replica_groups=mesh['dp'=32,'tensor'=4] {'tensor'}, dimensions={0} | all-to-all | bytes 2621440 | tf_op jit(solution)/shard_map/all_to_all | solution.py:33
  83.7 2.6 multiply_convert_fusion.3
  87.3 19.8 %all_to_all.36 = bf16[4,256,640]{2,1,0:T(8,128)(2,1)S(1)} all-to-all(bf16[4,256,640]{2,1,0:T(8,128)(2,1)S(1)} %bitcast.223), channel_id=1, replica_groups=mesh['dp'=32,'tensor'=4] {'tensor'}, dimensions={0} | all-to-all | bytes 2621440 | tf_op jit(solution)/shard_map/all_to_all | solution.py:21
  109.6 36.9 %all-gather.2.cloned.1.call-done = bf16[1024,1280]{1,0:T(8,128)(2,1)} async-done(((bf16[256,1280]{1,0:T(8,128)(2,1)}), bf16[1024,1280]{1,0:T(8,128)(2,1)}) %all-gather.2.cloned.1.call-update) | async-done | bytes 2621456 | tf_op jit(solution)/shard_map/all_gather | solution.py:42
  146.5 5.0 multiply_convert_fusion.2
  154.2 18.6 %all_to_all.37 = bf16[4,256,640]{2,1,0:T(8,128)(2,1)S(1)} all-to-all(bf16[4,256,640]{2,1,0:T(8,128)(2,1)S(1)} %bitcast.209), channel_id=1, replica_groups=mesh['dp'=32,'tensor'=4] {'tensor'}, dimensions={0} | all-to-all | bytes 2621440 | tf_op jit(solution)/shard_map/all_to_all | solution.py:21
  173.9 2.0 multiply_reduce_fusion.7
  176.1 1.2 broadcast_in_dim.61
  177.3 5.3 all-to-all-start.4
  182.6 3.0 convolution_convert_fusion.3
  185.6 1.7 convolution_convert_fusion.4
  187.9 1.9 convolution_convert_fusion.2
  189.8 9.4 %all-to-all-done.4 = bf16[4,256,640]{2,1,0:T(8,128)(2,1)} async-done(((bf16[4,256,640]{2,1,0:T(8,128)(2,1)}), bf16[4,256,640]{2,1,0:T(8,128)(2,1)}, u32[]{:S(2)}, u32[]{:S(2)}) %all-to-all-start.4) | async-done | bytes 1310752 | tf_op jit(solution)/shard_map/all_to_all | solution.py:33
  199.1 2.7 convolution_convert_fusion.7
  201.9 2.0 convolution_convert_fusion.5
  203.9 15.6 %while.29 = (s32[]{:T(128)}, f32[2,1,512,256]{3,2,1,0:T(8,128)S(1)}, f32[2,1024,256]{2,1,0:T(8,128)}, f32[2,1024,256]{2,1,0:T(8,128)}, s32[2,512]{1,0:T(2,128)S(...) while((s32[]{:T(128)}, ...), condition=%wide.region_18.19_spmd.clone, body=%wide.region_16.18_spmd.sunk.clone | while | flops 1349910528 | bytes 58758412 | solution.py:263
  205.4 1.2 multiply_reduce_fusion.18
  206.8 1.3 copy-done.18
  210.5 1.3 copy-done.22
  213.0 1.2 multiply_reduce_fusion.18
  214.4 1.3 copy-done.18
  218.2 1.3 copy-done.22
  219.5 2.3 fusion.94
  223.5 1.5 convolution_convert_fusion.8
  225.1 1.8 fusion.118
  226.9 1.2 slice.67
  229.2 2.3 fusion.100
  233.1 2.1 fusion.119
  236.3 3.5 add_convert_fusion
  239.8 5.4 all-to-all-start.5
  245.2 18.8 %all-to-all-done.5 = bf16[4,256,640]{2,1,0:T(8,128)(2,1)} async-done(((bf16[4,256,640]{2,1,0:T(8,128)(2,1)}), bf16[4,256,640]{2,1,0:T(8,128)(2,1)}, u32[]{:S(2)}, u32[]{:S(2)}) %all-to-all-start.5) | async-done | bytes 1310752 | tf_op jit(solution)/shard_map/all_to_all | solution.py:21
  264.1 1.6 convert_reduce_fusion
  266.2 1.2 broadcast_in_dim.101
  267.4 4.1 all-to-all-start.6
  271.5 2.7 fusion.113
  274.2 1.6 fusion.112
  275.8 2.5 slice.62
  278.3 71.3 %all-reduce.9 = (f32[640]{0:T(1024)}, f32[640]{0:T(1024)}, f32[640]{0:T(1024)}, f32[640]{0:T(1024)}, f32[256]{0:T(256)}, /*index=5*/f32[256]{0:T(256)}) all-reduce(f32[640]{0:T(1024)S(1)} %get-tuple-element.133, f32[640]{0:T(1024)S(1)} %copy-done.65, f32[640]{0:T(1024)S(1)} %copy-done.64, ...), channel_id=1, replica_groups=mesh['dp'=32,'tensor'=4] {'dp','tensor'}, use_global_device_ids=true, to_apply=%region_32.33 | all-reduce | flops 3072 | bytes 24576 | tf_op jit(solution)/shard_map/psum | solution.py:309
  349.6 226.8 %all-reduce.17.cloned.1.call-done = (bf16[640,256]{1,0:T(8,128)(2,1)}, bf16[256,640]{1,0:T(8,128)(2,1)}, bf16[640,512]{1,0:T(8,128)(2,1)}, bf16[640,512]{1,0:T(8,128)(2,1)}, bf16[512,640]{1,0:T(8,128)(2,1)}) async-done(((bf16[640,256]{1,0:T(8,128)(2,1)}, bf16[256,640]{1,0:T(8,128)(2,1)}, bf16[640,512]{1,0:T(8,128)(2,1)}, bf16[640,512]{1,0:T(8,128)(2,1)}, bf16[512,640]{1,0:T(8,128)(2,1)}), ...) | async-done | bytes 2621456 | tf_op jit(solution)/shard_map/psum | solution.py:303
  576.4 2.0 convert_element_type.173
  578.4 1.9 convert_element_type.175
  580.2 1.2 convert_element_type.177
  581.4 1.2 convert_element_type.179
  582.7 1.1 convert_element_type.181
  583.8 168.3 %all-reduce.15.cloned.1.call-done = (f32[640,256]{1,0:T(8,128)}, f32[640,256]{1,0:T(8,128)}) async-done(((f32[640,256]{1,0:T(8,128)}, f32[640,256]{1,0:T(8,128)}), (f32[640,256]{1,0:T(8,128)}, f32[640,256]{1,0:T(8,128)})) %all-reduce.15.cloned.1.call-update) | async-done | bytes 1310736 | tf_op jit(solution)/shard_map/psum | solution.py:309
  752.1 1.1 copy.71
  (274 shorter events, 32.9 us)
Async XLA Ops:
  7.2 79.1 %copy-start = (bf16[512,640]{1,0:T(8,128)(2,1)S(1)}, bf16[512,640]{1,0:T(8,128)(2,1)}, u32[]{:S(2)}) copy-start(bf16[512,640]{1,0:T(8,128)(2,1)} %param.31) | copy-start | bytes 1966084
  7.2 10.6 %copy-start.79 = (f32[128]{0:T(128)}, f32[128]{0:T(128)S(1)}, u32[]{:S(2)}) copy-start(f32[128]{0:T(128)S(1)} %multiply_power_fusion) | copy-start | bytes 1540
  11.1 2.2 copy-start.9
  11.1 2.2 copy-start.44
  11.1 2.2 copy-start.61
  11.1 3.0 copy-start.81
  14.9 2.7 copy-start.68
  14.9 2.9 copy-start.4
  15.0 2.7 copy-start.70
  15.0 2.6 copy-start.48
  35.2 22.2 %all-to-all-start = ((bf16[4,256,640]{2,1,0:T(8,128)(2,1)}), bf16[4,256,640]{2,1,0:T(8,128)(2,1)}, u32[]{:S(2)}, u32[]{:S(2)}) async-start(bf16[4,256,640]{2,1,0:T(8,128)(2,1)} %bitcast.29), calls=%async_computation | async-start | bytes 2621440 | tf_op jit(solution)/shard_map/all_to_all | solution.py:21
  40.9 105.6 %all-gather.2.cloned.1.call-start = ((), (), s32[]{:S(2)}) async-start(), calls=%async_computation.7 | async-start | bytes 3276800 | tf_op jit(solution)/shard_map/all_gather | solution.py:42
  57.4 4.8 copy-start.50
  59.6 2.0 copy-start.56
  62.3 19.8 %copy-start.36 = (bf16[640,512]{1,0:T(8,128)(2,1)S(1)}, bf16[640,512]{1,0:T(8,128)(2,1)}, u32[]{:S(2)}) copy-start(bf16[640,512]{1,0:T(8,128)(2,1)} %param.29) | copy-start | bytes 1966084
  83.7 2.6 copy-start.83
  86.3 20.9 %copy-start.84 = (bf16[1024,512]{1,0:T(8,128)(2,1)}, bf16[1024,512]{1,0:T(8,128)(2,1)S(1)}, u32[]{:S(2)}) copy-start(bf16[1024,512]{1,0:T(8,128)(2,1)S(1)} %get-tuple-element.220) | copy-start | bytes 3145732
  87.3 20.2 %copy-start.29 = (bf16[1024,640]{1,0:T(8,128)(2,1)S(1)}, bf16[1024,640]{1,0:T(8,128)(2,1)}, u32[]{:S(2)}) copy-start(bf16[1024,640]{1,0:T(8,128)(2,1)} %param.24) | copy-start | bytes 3932164
  87.3 20.2 %copy-start.60 = (f32[640]{0:T(1024)S(1)}, f32[640]{0:T(1024)}, u32[]{:S(2)}) copy-start(f32[640]{0:T(1024)} %param.35) | copy-start | bytes 7684
  146.5 5.1 copy-start.37
  154.2 18.9 %copy-start.51 = (f32[640]{0:T(1024)S(1)}, f32[640]{0:T(1024)}, u32[]{:S(2)}) copy-start(f32[640]{0:T(1024)} %param.34) | copy-start | bytes 7684
  154.2 18.9 %copy-start.59 = (f32[256]{0:T(256)S(1)}, f32[256]{0:T(256)}, u32[]{:S(2)}) copy-start(f32[256]{0:T(256)} %copy-done.58) | copy-start | bytes 3076
  173.1 2.9 copy-start.76
  176.1 6.5 copy-start.17
  177.3 21.8 %all-to-all-start.4 = ((bf16[4,256,640]{2,1,0:T(8,128)(2,1)}), bf16[4,256,640]{2,1,0:T(8,128)(2,1)}, u32[]{:S(2)}, u32[]{:S(2)}) async-start(bf16[4,256,640]{2,1,0:T(8,128)(2,1)} %broadcast_in_dim.61), calls=%async_computation.4 | async-start | bytes 2621440 | tf_op jit(solution)/shard_map/all_to_all | solution.py:33
  182.6 393.8 %all-reduce.17.cloned.1.call-start = ((), (), s32[]{:S(2)}) async-start(), calls=%async_computation.9 | async-start | bytes 5242880 | tf_op jit(solution)/shard_map/psum | solution.py:303
  182.6 3.0 copy-start.27
  185.6 1.7 copy-start.30
  185.6 2.2 copy-start.85
  199.1 2.8 copy-start.41
  199.1 4.7 copy-start.24
  199.1 4.8 copy-start.55
  201.9 2.0 copy-start.40
  203.9 15.6 %copy-start.80 = (f32[128]{0:T(128)S(1)}, f32[128]{0:T(128)}, u32[]{:S(2)}) copy-start(f32[128]{0:T(128)} %copy-done.79) | copy-start | bytes 1540
  208.1 1.9 copy-start.21
  208.6 1.8 copy-start.19
  215.8 1.9 copy-start.21
  216.3 1.8 copy-start.19
  219.5 2.3 copy-start.5
  219.5 2.3 copy-start.49
  219.5 2.3 copy-start.71
  219.5 2.8 copy-start.69
  225.1 3.0 copy-start.20
  226.9 2.1 copy-start.23
  229.0 2.4 copy-start.3
  229.0 2.4 copy-start.47
  229.0 2.4 copy-start.73
  229.1 2.8 copy-start.67
  239.8 5.4 copy-start.74
  239.8 25.9 %copy-start.6 = (f32[1024,640]{1,0:T(8,128)S(1)}, f32[1024,640]{1,0:T(8,128)}, u32[]{:S(2)}) copy-start(f32[1024,640]{1,0:T(8,128)} %convert_element_type.144) | copy-start | bytes 7864324
  239.8 24.3 %all-to-all-start.5 = ((bf16[4,256,640]{2,1,0:T(8,128)(2,1)}), bf16[4,256,640]{2,1,0:T(8,128)(2,1)}, u32[]{:S(2)}, u32[]{:S(2)}) async-start(bf16[4,256,640]{2,1,0:T(8,128)(2,1)} %bitcast.207), calls=%async_computation.5 | async-start | bytes 2621440 | tf_op jit(solution)/shard_map/all_to_all | solution.py:21
  245.2 20.7 %copy-start.8 = (f32[256,640]{1,0:T(8,128)S(1)}, f32[256,640]{1,0:T(8,128)}, u32[]{:S(2)}) copy-start(f32[256,640]{1,0:T(8,128)} %copy-done.7) | copy-start | bytes 1966084
  266.2 5.3 copy-start.11
  267.4 82.3 %all-to-all-start.6 = ((bf16[4,256,640]{2,1,0:T(8,128)(2,1)}), bf16[4,256,640]{2,1,0:T(8,128)(2,1)S(1)}, u32[]{:S(2)}, u32[]{:S(2)}) async-start(bf16[4,256,640]{2,1,0:T(8,128)(2,1)} %broadcast_in_dim.101), calls=%async_computation.6 | async-start | bytes 2621440 | tf_op jit(solution)/shard_map/all_to_all | solution.py:33
  271.5 2.7 copy-start.13
  271.5 480.7 %all-reduce.15.cloned.1.call-start = ((), (), s32[]{:S(2)}) async-start(), calls=%async_computation.8 | async-start | bytes 2621440 | tf_op jit(solution)/shard_map/psum | solution.py:309
  275.7 2.5 copy-start.63
  275.7 2.5 copy-start.64
  275.7 2.5 copy-start.65
  576.4 3.8 copy-start.35
  576.4 5.0 copy-start.34
  580.2 2.5 copy-start.33
  752.1 2.4 copy-start.31
  752.1 3.2 copy-start.1
  (36 other events, 43.0 us)
Sparse Core Ops, SparseCore 0:
  109.7 36.6 all-gather.1
  235.4 340.9 all-reduce.16
  581.9 170.1 all-reduce.14
where the time goes:
time: 763 us; the launch traced here: 762 us
  waiting for transfers between devices  475 us (62%)
  blocking collectives  129 us (17%)
  matrix products  55.3 us (7%)
  other arithmetic  39.8 us (5%)
  local copies, waits for them, and re-layouts  26.5 us (3%)
  starting transfers between devices  20.5 us (3%)
  between operations  14.7 us (2%)
    psum x1, waiting for transfers between devices, local(): lax.psum(grad_query.astype(jnp.bfloat16), 'dp').astype(jnp.float32)  227 us
    psum x1, waiting for transfers between devices, local(): lax.psum((grad_key, grad_value, grad_attn_in, grad_attn_out, grad_ffn_in,...  168 us
    psum x1, blocking collectives, local(): lax.psum((grad_key, grad_value, grad_attn_in, grad_attn_out, grad_ffn_in,...  71.3 us
    all_to_all x2, blocking collectives, sum_at_owner(): tiles = lax.all_to_all(in_blocks(x, dim, size), axis, 0, 0, tiled=True)  38.5 us
    all_gather x1, waiting for transfers between devices, in_one_piece(): lax.all_gather(both, axis, axis=dim, tiled=True)  36.9 us
    all_to_all x2, waiting for transfers between devices, sum_at_owner(): tiles = lax.all_to_all(in_blocks(x, dim, size), axis, 0, 0, tiled=True)  33.7 us
    all_to_all x1, blocking collectives, copy_for_each(): return lax.all_to_all(copies, axis, split_axis=0, concat_axis=0, tiled=True)  19.7 us
  transfers between devices with their start and end apart: 7, of which 6 were waited for; matrix products, arithmetic and copies ran while one was open for 4% of the time, Pallas kernels for 0%

commit v1 on v0

--- a/solution.py
+++ b/solution.py
@@ -300,7 +300,7 @@
     grad_ffn_in = gain_term(gain_inputs[4], gain_inputs[5])
     grad_ffn_out = gain_term(gain_inputs[6], gain_inputs[7])
     grad_query, grad_out, grad_gate, grad_up, grad_down = (
-        lax.psum(grad_query.astype(jnp.bfloat16), "dp").astype(jnp.float32),
+        jnp.sum(lax.all_gather(grad_query.astype(jnp.bfloat16), "dp"), axis=0).astype(jnp.float32),
         lax.psum(grad_out.astype(jnp.bfloat16), "dp").astype(jnp.float32),
         lax.psum(grad_gate.astype(jnp.bfloat16), "dp").astype(jnp.float32),
         lax.psum(grad_up.astype(jnp.bfloat16), "dp").astype(jnp.float32),

time: 763 us -> 849 us (1.11)
  waiting for transfers between devices: 475 us -> 560 us
    all_gather x0 -> x1, waiting for transfers between devices: none -> 135 us  [local(): lax.all_gather(grad_query.astype(jnp.bfloat16), 'dp')]
    psum x1, waiting for transfers between devices: 227 us -> 200 us  [local(): lax.psum(grad_out.astype(jnp.bfloat16), 'dp').astype(jnp.float32)]
    psum x1, waiting for transfers between devices: 168 us -> 146 us  [local(): lax.psum((grad_key, grad_value, grad_attn_in, grad_attn_out, grad_ffn_in,...]
  transfers between devices with their start and end apart: 7 -> 8, of which waited for: 6 -> 7; matrix products, arithmetic and copies ran while one was open for 4% -> 6% of each run, Pallas kernels for 0% -> 0%
where the time goes in v1:
time: 849 us; the launch traced here: 848 us
  waiting for transfers between devices  560 us (66%)
  blocking collectives  128 us (15%)
  matrix products  50.7 us (6%)
  other arithmetic  47.5 us (6%)
  local copies, waits for them, and re-layouts  26.5 us (3%)
  starting transfers between devices  19.9 us (2%)
  between operations  14.6 us (2%)
    psum x1, waiting for transfers between devices, local(): lax.psum(grad_out.astype(jnp.bfloat16), 'dp').astype(jnp.float32)  200 us
    psum x1, waiting for transfers between devices, local(): lax.psum((grad_key, grad_value, grad_attn_in, grad_attn_out, grad_ffn_in,...  146 us
    all_gather x1, waiting for transfers between devices, local(): lax.all_gather(grad_query.astype(jnp.bfloat16), 'dp')  135 us
    psum x1, blocking collectives, local(): lax.psum((grad_key, grad_value, grad_attn_in, grad_attn_out, grad_ffn_in,...  70.1 us
    all_to_all x2, blocking collectives, sum_at_owner(): tiles = lax.all_to_all(in_blocks(x, dim, size), axis, 0, 0, tiled=True)  38.5 us
    all_gather x1, waiting for transfers between devices, in_one_piece(): lax.all_gather(both, axis, axis=dim, tiled=True)  36.8 us
    all_to_all x2, waiting for transfers between devices, sum_at_owner(): tiles = lax.all_to_all(in_blocks(x, dim, size), axis, 0, 0, tiled=True)  33.4 us
    all_to_all x1, blocking collectives, copy_for_each(): return lax.all_to_all(copies, axis, split_axis=0, concat_axis=0, tiled=True)  19.7 us
  transfers between devices with their start and end apart: 8, of which 7 were waited for; matrix products, arithmetic and copies ran while one was open for 6% of the time, Pallas kernels for 0%

profile of v1, /device:TPU:1, one launch (start us, length us, event | category | flops | bytes accessed | tf_op | source)
XLA Modules:
  0.0 847.7 jit_solution(17462549218330773450)
XLA Ops:
  9.8 1.6 multiply_reduce_fusion.1
  11.5 2.1 convolution_convert_fusion.6
  15.7 2.4 fusion.97
  18.3 2.4 fusion.91
  20.7 1.1 fusion.60
  22.7 10.4 %while.28 = (s32[]{:T(128)}, bf16[2,1,512,256]{3,2,1,0:T(8,128)(2,1)S(1)}, f32[2,1,512]{2,1,0:T(1,128)}, s32[2,512]{1,0:T(2,128)S(1)}, s32[2,1024]{1,0:T(2,128)S...) while((s32[]{:T(128)}, ...), condition=%wide.region_6.7_spmd.clone, body=%wide.region_3.6_spmd.sunk.clone | while | flops 552075264 | bytes 8220833 | solution.py:212
  22.7 2.0 fusion.189
  25.8 1.4 fusion.191
  27.9 2.0 fusion.189
  30.9 1.4 fusion.191
  33.0 2.6 convolution_convert_fusion
  35.6 5.7 all-to-all-start
  41.3 1.8 convert_element_type.146
  43.1 14.8 %all-to-all-done = bf16[4,256,640]{2,1,0:T(8,128)(2,1)} async-done(((bf16[4,256,640]{2,1,0:T(8,128)(2,1)}), bf16[4,256,640]{2,1,0:T(8,128)(2,1)}, u32[]{:S(2)}, u32[]{:S(2)}) %all-to-all-start) | async-done | bytes 1310752 | tf_op jit(solution)/shard_map/all_to_all | solution.py:21
  57.8 1.6 convert_reduce_fusion.3
  60.1 2.0 multiply_reduce_fusion.14
  62.9 19.7 %all_to_all.35 = bf16[4,256,640]{2,1,0:T(8,128)(2,1)S(1)} all-to-all(bf16[4,256,640]{2,1,0:T(8,128)(2,1)S(1)} %broadcast_in_dim.57), channel_id=1, replica_groups=mesh['dp'=32,'tensor'=4] {'tensor'}, dimensions={0} | all-to-all | bytes 2621440 | tf_op jit(solution)/shard_map/all_to_all | solution.py:33
  84.1 2.6 multiply_convert_fusion.3
  87.8 19.8 %all_to_all.36 = bf16[4,256,640]{2,1,0:T(8,128)(2,1)S(1)} all-to-all(bf16[4,256,640]{2,1,0:T(8,128)(2,1)S(1)} %bitcast.224), channel_id=1, replica_groups=mesh['dp'=32,'tensor'=4] {'tensor'}, dimensions={0} | all-to-all | bytes 2621440 | tf_op jit(solution)/shard_map/all_to_all | solution.py:21
  110.1 36.8 %all-gather.4.cloned.1.call-done = bf16[1024,1280]{1,0:T(8,128)(2,1)} async-done(((bf16[256,1280]{1,0:T(8,128)(2,1)}), bf16[1024,1280]{1,0:T(8,128)(2,1)}) %all-gather.4.cloned.1.call-update) | async-done | bytes 2621456 | tf_op jit(solution)/shard_map/all_gather | solution.py:42
  146.9 5.0 multiply_convert_fusion.2
  154.6 18.6 %all_to_all.37 = bf16[4,256,640]{2,1,0:T(8,128)(2,1)S(1)} all-to-all(bf16[4,256,640]{2,1,0:T(8,128)(2,1)S(1)} %bitcast.210), channel_id=1, replica_groups=mesh['dp'=32,'tensor'=4] {'tensor'}, dimensions={0} | all-to-all | bytes 2621440 | tf_op jit(solution)/shard_map/all_to_all | solution.py:21
  174.4 2.0 multiply_reduce_fusion.7
  176.6 1.2 broadcast_in_dim.61
  177.7 5.3 all-to-all-start.4
  183.0 3.0 convolution_convert_fusion.3
  186.1 1.7 convolution_convert_fusion.4
  188.3 1.9 convolution_convert_fusion.2
  190.2 9.3 %all-to-all-done.4 = bf16[4,256,640]{2,1,0:T(8,128)(2,1)} async-done(((bf16[4,256,640]{2,1,0:T(8,128)(2,1)}), bf16[4,256,640]{2,1,0:T(8,128)(2,1)}, u32[]{:S(2)}, u32[]{:S(2)}) %all-to-all-start.4) | async-done | bytes 1310752 | tf_op jit(solution)/shard_map/all_to_all | solution.py:33
  199.5 2.6 convolution_convert_fusion.7
  202.2 2.1 convolution_convert_fusion.5
  204.6 15.3 %while.29 = (s32[]{:T(128)}, f32[2,1,512,256]{3,2,1,0:T(8,128)S(1)}, f32[2,1024,256]{2,1,0:T(8,128)}, f32[2,1024,256]{2,1,0:T(8,128)}, s32[2,512]{1,0:T(2,128)S(...) while((s32[]{:T(128)}, ...), condition=%wide.region_18.19_spmd.clone, body=%wide.region_16.18_spmd.sunk.clone | while | flops 1349910528 | bytes 58758412 | solution.py:263
  205.8 1.2 multiply_reduce_fusion.18
  207.3 1.3 copy-done.14
  211.0 1.3 copy-done.18
  213.5 1.2 multiply_reduce_fusion.18
  214.9 1.3 copy-done.14
  218.6 1.3 copy-done.18
  220.0 2.3 fusion.94
  223.6 1.5 convolution_convert_fusion.8
  225.1 1.1 slice.67
  226.2 1.1 slice.65
  227.3 1.4 slice_add_fusion.1
  228.8 2.3 fusion.100
  234.7 1.7 add_convert_fusion
  236.4 4.5 all-to-all-start.5
  240.9 18.7 %all-to-all-done.5 = bf16[4,256,640]{2,1,0:T(8,128)(2,1)S(1)} async-done(((bf16[4,256,640]{2,1,0:T(8,128)(2,1)}), bf16[4,256,640]{2,1,0:T(8,128)(2,1)S(1)}, u32[]{:S(2)}, u32[]{:S(2)}) %all-to-all-start.5) | async-done | bytes 1310752 | tf_op jit(solution)/shard_map/all_to_all | solution.py:21
  259.7 1.3 multiply_reduce_fusion.8
  261.0 1.3 fusion.89
  262.3 1.2 broadcast_in_dim.101
  263.5 4.2 all-to-all-start.6
  267.7 2.6 fusion.113
  270.3 1.6 fusion.112
  271.9 2.5 slice.62
  274.4 70.1 %all-reduce.9 = (f32[640]{0:T(1024)}, f32[640]{0:T(1024)}, f32[640]{0:T(1024)}, f32[640]{0:T(1024)}, f32[256]{0:T(256)}, /*index=5*/f32[256]{0:T(256)}) all-reduce(f32[640]{0:T(1024)S(1)} %get-tuple-element.133, f32[640]{0:T(1024)S(1)} %copy-done.59, f32[640]{0:T(1024)S(1)} %copy-done.58, ...), channel_id=1, replica_groups=mesh['dp'=32,'tensor'=4] {'dp','tensor'}, use_global_device_ids=true, to_apply=%region_32.33 | all-reduce | flops 3072 | bytes 24576 | tf_op jit(solution)/shard_map/psum | solution.py:309
  344.5 200.2 %all-reduce.17.cloned.1.call-done = (bf16[256,640]{1,0:T(8,128)(2,1)}, bf16[640,512]{1,0:T(8,128)(2,1)}, bf16[640,512]{1,0:T(8,128)(2,1)}, bf16[512,640]{1,0:T(8,128)(2,1)}) async-done(((bf16[256,640]{1,0:T(8,128)(2,1)}, bf16[640,512]{1,0:T(8,128)(2,1)}, bf16[640,512]{1,0:T(8,128)(2,1)}, bf16[512,640]{1,0:T(8,128)(2,1)}), (bf16[256,640]{1,0:T(8,128)(2,1)}, bf16[640,512]{1,0:T(8,128)(2,1)}, ...) | async-done | bytes 2293776 | tf_op jit(solution)/shard_map/psum | solution.py:304
  544.7 1.9 convert_element_type.177
  546.6 2.4 convert_element_type.179
  549.0 1.2 convert_element_type.181
  550.2 1.1 convert_element_type.183
  551.4 134.5 %all-gather.6.cloned.1.call-done = bf16[20480,256]{1,0:T(8,128)(2,1)} async-done(((bf16[640,256]{1,0:T(8,128)(2,1)}), bf16[20480,256]{1,0:T(8,128)(2,1)}) %all-gather.6.cloned.1.call-update) | async-done | bytes 10485776 | tf_op jit(solution)/shard_map/all_gather | solution.py:303
  685.9 5.7 reduce_sum.263
  692.4 145.5 %all-reduce.15.cloned.1.call-done = (f32[640,256]{1,0:T(8,128)}, f32[640,256]{1,0:T(8,128)}) async-done(((f32[640,256]{1,0:T(8,128)}, f32[640,256]{1,0:T(8,128)}), (f32[640,256]{1,0:T(8,128)}, f32[640,256]{1,0:T(8,128)})) %all-reduce.15.cloned.1.call-update) | async-done | bytes 1310736 | tf_op jit(solution)/shard_map/psum | solution.py:309
  837.9 1.1 copy.70
  (266 shorter events, 35.8 us)
Async XLA Ops:
  7.2 79.6 %copy-start = (bf16[512,640]{1,0:T(8,128)(2,1)S(1)}, bf16[512,640]{1,0:T(8,128)(2,1)}, u32[]{:S(2)}) copy-start(bf16[512,640]{1,0:T(8,128)(2,1)} %param.31) | copy-start | bytes 1966084
  11.5 2.2 copy-start.8
  11.5 2.2 copy-start.38
  11.5 2.2 copy-start.55
  11.5 3.0 copy-start.75
  15.4 2.7 copy-start.62
  15.4 2.9 copy-start.4
  15.4 2.7 copy-start.64
  15.4 2.7 copy-start.42
  35.6 22.2 %all-to-all-start = ((bf16[4,256,640]{2,1,0:T(8,128)(2,1)}), bf16[4,256,640]{2,1,0:T(8,128)(2,1)}, u32[]{:S(2)}, u32[]{:S(2)}) async-start(bf16[4,256,640]{2,1,0:T(8,128)(2,1)} %bitcast.29), calls=%async_computation | async-start | bytes 2621440 | tf_op jit(solution)/shard_map/all_to_all | solution.py:21
  41.3 105.6 %all-gather.4.cloned.1.call-start = ((), (), s32[]{:S(2)}) async-start(), calls=%async_computation.7 | async-start | bytes 3276800 | tf_op jit(solution)/shard_map/all_gather | solution.py:42
  57.8 4.8 copy-start.44
  60.1 2.0 copy-start.50
  62.8 19.8 %copy-start.30 = (bf16[640,512]{1,0:T(8,128)(2,1)S(1)}, bf16[640,512]{1,0:T(8,128)(2,1)}, u32[]{:S(2)}) copy-start(bf16[640,512]{1,0:T(8,128)(2,1)} %param.29) | copy-start | bytes 1966084
  82.6 1.6 copy-start.32
  84.1 2.6 copy-start.77
  86.8 20.9 %copy-start.78 = (bf16[1024,512]{1,0:T(8,128)(2,1)}, bf16[1024,512]{1,0:T(8,128)(2,1)S(1)}, u32[]{:S(2)}) copy-start(bf16[1024,512]{1,0:T(8,128)(2,1)S(1)} %get-tuple-element.219) | copy-start | bytes 3145732
  87.8 20.2 %copy-start.24 = (bf16[1024,640]{1,0:T(8,128)(2,1)S(1)}, bf16[1024,640]{1,0:T(8,128)(2,1)}, u32[]{:S(2)}) copy-start(bf16[1024,640]{1,0:T(8,128)(2,1)} %param.24) | copy-start | bytes 3932164
  87.8 20.2 %copy-start.54 = (f32[640]{0:T(1024)S(1)}, f32[640]{0:T(1024)}, u32[]{:S(2)}) copy-start(f32[640]{0:T(1024)} %param.35) | copy-start | bytes 7684
  146.9 5.1 copy-start.31
  152.0 1.6 copy-start.33
  154.6 18.9 %copy-start.45 = (f32[640]{0:T(1024)S(1)}, f32[640]{0:T(1024)}, u32[]{:S(2)}) copy-start(f32[640]{0:T(1024)} %param.34) | copy-start | bytes 7684
  154.6 18.9 %copy-start.53 = (f32[256]{0:T(256)S(1)}, f32[256]{0:T(256)}, u32[]{:S(2)}) copy-start(f32[256]{0:T(256)} %copy-done.52) | copy-start | bytes 3076
  173.5 2.9 copy-start.70
  176.6 6.5 copy-start.13
  177.7 21.8 %all-to-all-start.4 = ((bf16[4,256,640]{2,1,0:T(8,128)(2,1)}), bf16[4,256,640]{2,1,0:T(8,128)(2,1)}, u32[]{:S(2)}, u32[]{:S(2)}) async-start(bf16[4,256,640]{2,1,0:T(8,128)(2,1)} %broadcast_in_dim.61), calls=%async_computation.4 | async-start | bytes 2621440 | tf_op jit(solution)/shard_map/all_to_all | solution.py:33
  183.0 361.6 %all-reduce.17.cloned.1.call-start = ((), (), s32[]{:S(2)}) async-start(), calls=%async_computation.10 | async-start | bytes 4587520 | tf_op jit(solution)/shard_map/psum | solution.py:304
  183.0 3.0 copy-start.22
  186.1 1.7 copy-start.25
  186.1 2.2 copy-start.79
  202.2 2.4 copy-start.19
  202.2 2.4 copy-start.34
  202.2 2.4 copy-start.49
  204.3 481.6 %all-gather.6.cloned.1.call-start = ((), (), s32[]{:S(2)}) async-start(), calls=%async_computation.8 | async-start | bytes 10813440 | tf_op jit(solution)/shard_map/all_gather | solution.py:303
  204.6 15.4 %copy-start.74 = (f32[128]{0:T(128)S(1)}, f32[128]{0:T(128)}, u32[]{:S(2)}) copy-start(f32[128]{0:T(128)} %multiply_power_fusion) | copy-start | bytes 1540
  207.0 1.6 copy-start.14
  208.6 1.9 copy-start.17
  209.1 1.8 copy-start.15
  214.7 1.6 copy-start.14
  216.3 1.9 copy-start.17
  216.8 1.8 copy-start.15
  219.9 2.3 copy-start.5
  219.9 2.3 copy-start.43
  219.9 2.3 copy-start.65
  220.0 2.8 copy-start.63
  227.3 3.8 copy-start.3
  227.3 3.8 copy-start.41
  227.3 3.8 copy-start.67
  228.8 2.8 copy-start.61
  228.8 2.8 copy-start.16
  236.4 4.5 copy-start.68
  236.4 23.2 %all-to-all-start.5 = ((bf16[4,256,640]{2,1,0:T(8,128)(2,1)}), bf16[4,256,640]{2,1,0:T(8,128)(2,1)S(1)}, u32[]{:S(2)}, u32[]{:S(2)}) async-start(bf16[4,256,640]{2,1,0:T(8,128)(2,1)} %bitcast.44), calls=%async_computation.5 | async-start | bytes 2621440 | tf_op jit(solution)/shard_map/all_to_all | solution.py:21
  240.9 20.1 %copy-start.7 = (f32[256,640]{1,0:T(8,128)S(1)}, f32[256,640]{1,0:T(8,128)}, u32[]{:S(2)}) copy-start(f32[256,640]{1,0:T(8,128)} %copy-done.6) | copy-start | bytes 1966084
  262.3 5.4 copy-start.10
  263.5 81.0 %all-to-all-start.6 = ((bf16[4,256,640]{2,1,0:T(8,128)(2,1)}), bf16[4,256,640]{2,1,0:T(8,128)(2,1)S(1)}, u32[]{:S(2)}, u32[]{:S(2)}) async-start(bf16[4,256,640]{2,1,0:T(8,128)(2,1)} %broadcast_in_dim.101), calls=%async_computation.6 | async-start | bytes 2621440 | tf_op jit(solution)/shard_map/all_to_all | solution.py:33
  267.7 570.3 %all-reduce.15.cloned.1.call-start = ((), (), s32[]{:S(2)}) async-start(), calls=%async_computation.9 | async-start | bytes 2621440 | tf_op jit(solution)/shard_map/psum | solution.py:309
  271.9 2.5 copy-start.57
  271.9 2.5 copy-start.58
  271.9 2.5 copy-start.59
  544.7 4.3 copy-start.29
  546.6 3.6 copy-start.28
  837.9 1.5 copy-start.27
  837.9 2.4 copy-start.26
  837.9 3.2 copy-start.1
  (31 other events, 33.2 us)
Sparse Core Ops, SparseCore 0:
  110.2 36.6 all-gather.3
  204.4 340.2 all-reduce.16
  548.4 137.4 all-gather.5
  691.3 146.6 all-reduce.14
